TPU v7x, 128 devices: a whole 4x4x4 slice. The times are simulated.
128 devices in a mesh: tile: 32 (over z, x, core), frame: 4 (over y).
Axes of the slice: x: 4, y: 4, z: 4, core: 2. Of those that a mesh axis runs over, the one named last changes fastest.
Arguments:
- cells: bfloat16 [4, 65536, 128], P('frame', 'tile'), may hold values from -24 to 24
- vectors: bfloat16 [8, 128], replicated, may hold values from -6 to 6
- weights: bfloat16 [4, 128, 128], replicated, may hold values from -0.5 to 0.5
- cuboid_shift: int32 [1], replicated, may hold values from 0 to 2047
- cell_upstream: bfloat16 [4, 65536, 128], P('frame', 'tile'), may hold values from -6 to 6
- vector_upstream: float32 [8, 128], replicated, may hold values from -6 to 6
Outputs:
- cell_grad: bfloat16 [4, 65536, 128], P('frame', 'tile')
- weight_grad: float32 [4, 128, 128], replicated
- vector_grad: float32 [8, 128], replicated
All inputs are finite; a program needn't handle non-finite values.
Results may differ from a plain program's by a relative error of at most 0.008.
The roundings to bfloat16 on the way count: a program that leaves them out, or rounds other values in their place, can miss the bound.
Values may be sent and summed in bfloat16 or wider, within the bound.
No kernel may reach another device: no remote copies, remote signals or barrier semaphores. Data moves between devices by JAX's collectives and lax.ppermute only.
A program may use at most 64 MiB of HBM per device.

v0:
```python
import math

import jax
import jax.numpy as jnp
from jax import lax
from jax.experimental import pallas as pl
from jax.experimental.pallas import tpu as pltpu
from jax.sharding import PartitionSpec as P

CH = 128
HEADS = 4
HDIM = 32
GLOBALS = 8
PAIRS = HEADS * GLOBALS
SPAN = 4
CELLS_DEV = 2048
PEERS = 128
PEER_ROWS = CELLS_DEV // PEERS
CUBOIDS = PEER_ROWS // SPAN
TOKENS = 512
QUERIES = 256
GROUP = 16
GROUP_ROWS = GROUP * PEER_ROWS
WINDOW = GROUP_ROWS + 16
MSG_SPANS = 9
PIECE_ROWS = 2 * SPAN
PIECE_GROUP = 32
VEC_LANES = 2 * GLOBALS
SCALE = HDIM**-0.5
LOG2E = math.log2(math.e)
BF = jnp.bfloat16
F32 = jnp.float32
NT = (((1,), (1,)), ((), ()))


def dot(a, b):
    return jnp.dot(a, b, preferred_element_type=F32)


def dot_nt(a, b):
    return lax.dot_general(a, b, NT, preferred_element_type=F32)


def iota(shape, axis):
    return lax.broadcasted_iota(jnp.int32, shape, axis)


def split3(x):
    hi = x.astype(BF)
    rest = x - hi.astype(F32)
    mid = rest.astype(BF)
    low = (rest - mid.astype(F32)).astype(BF)
    return hi, mid, low


def head_blocks(rows):
    head = iota((GLOBALS, CH), 1) // HDIM
    return jnp.concatenate([jnp.where(head == h, rows, 0.0) for h in range(HEADS)], axis=0)


def diagonal(first, second):
    zero = jnp.zeros((CH, CH), F32)
    rows = [jnp.concatenate([first, zero], axis=1), jnp.concatenate([zero, second], axis=1)]
    return jnp.concatenate(rows, axis=0).astype(BF)


def head_diagonal(blocks):
    head = iota((GLOBALS, CH), 1) // HDIM
    total = jnp.zeros((GLOBALS, CH), F32)
    for h in range(HEADS):
        total += jnp.where(head == h, blocks[h * GLOBALS : (h + 1) * GLOBALS], 0.0)
    return total


def global_rows(vectors, weight):
    return dot(vectors.astype(BF), weight).astype(BF).astype(F32)


def global_upstream(vector_upstream, w_out):
    hi, mid, low = split3(vector_upstream)
    return dot_nt(hi, w_out) + dot_nt(mid, w_out) + dot_nt(low, w_out)


def tile_offset(shift_ref):
    return (shift_ref[0] * (lax.axis_index("tile") + 1)) % CELLS_DEV


def shift_matrix(step, rows, window):
    return (iota((rows, window), 1) == iota((rows, window), 0) + step).astype(BF)


def pack_kernel(
    shift_hbm,
    cells_hbm,
    up_hbm,
    vectors_hbm,
    weights_hbm,
    vup_hbm,
    msg_ref,
    held,
    vectors_ref,
    weights_ref,
    vup_ref,
    shift_ref,
    sems,
):
    whole, wrap = pl.ds(0, CELLS_DEV), pl.ds(CELLS_DEV, WINDOW)
    left, right = pl.ds(0, CH), pl.ds(CH, CH)
    copies = [
        pltpu.make_async_copy(source, target, sems.at[i])
        for i, (source, target) in enumerate(
            [
                (vectors_hbm, vectors_ref),
                (weights_hbm, weights_ref),
                (vup_hbm, vup_ref),
                (cells_hbm, held.at[whole, left]),
                (cells_hbm.at[pl.ds(0, WINDOW)], held.at[wrap, left]),
                (up_hbm, held.at[whole, right]),
                (up_hbm.at[pl.ds(0, WINDOW)], held.at[wrap, right]),
                (shift_hbm, shift_ref),
            ]
        )
    ]
    for copy in copies:
        copy.start()
    for copy in copies[:5]:
        copy.wait()
    vectors = vectors_ref[...].astype(F32)
    cells = held[:CELLS_DEV, :CH]
    query = head_blocks(global_rows(vectors, weights_ref[0])).astype(BF)
    upstream = head_blocks(global_upstream(vup_ref[...], weights_ref[3]))
    up_parts = jnp.concatenate([part.astype(F32) for part in split3(upstream)], axis=0).astype(BF)
    w_kv = jnp.concatenate([weights_ref[1], weights_ref[2]], axis=1)
    key_value = dot(cells, w_kv).astype(BF)
    score = dot_nt(query, key_value[:, :CH]) * SCALE
    dprob = dot_nt(up_parts, key_value[:, CH:])
    dprob = dprob[:PAIRS] + dprob[PAIRS : 2 * PAIRS] + dprob[2 * PAIRS :]
    top = jnp.max(score, axis=1, keepdims=True)
    weight = jnp.exp(score - top)
    total = jnp.sum(weight, axis=1, keepdims=True)
    inner = jnp.sum(weight * dprob, axis=1, keepdims=True)
    lane = iota((PAIRS, CH), 1)
    stats = jnp.where(lane == 0, top, jnp.where(lane == 1, total, jnp.where(lane == 2, inner, 0.0)))
    parts = [part.astype(F32) for part in split3(stats)] + [jnp.zeros((PAIRS, CH), F32)]
    rows = jnp.concatenate(parts, axis=0).T[:GLOBALS].astype(BF)
    msg_ref[:, 2 * CUBOIDS] = jnp.broadcast_to(rows[None, :SPAN], (PEERS, SPAN, CH))
    for copy in copies[5:]:
        copy.wait()
    offset = tile_offset(shift_ref)
    base = offset - offset % 16
    mover = shift_matrix(offset % 16, GROUP_ROWS - 16, GROUP_ROWS)
    for first in range(0, PEERS, GROUP - 1):
        count = min(GROUP - 1, PEERS - first)
        start = pl.multiple_of((base + first * PEER_ROWS) % CELLS_DEV, 16)
        rows = held[pl.ds(start, GROUP_ROWS), :]
        moved = dot(mover[: count * PEER_ROWS], rows).astype(BF)
        peers = pl.ds(first, count)
        shape = (count, CUBOIDS, SPAN, CH)
        msg_ref[peers, 0:CUBOIDS] = moved[:, :CH].reshape(shape)
        msg_ref[peers, CUBOIDS : 2 * CUBOIDS] = moved[:, CH:].reshape(shape)


def piece_matrix():
    rows = PIECE_GROUP * PIECE_ROWS
    row = iota((rows, rows), 0)
    source = row // SPAN % 2 * CH + row // PIECE_ROWS * SPAN + row % SPAN
    return (iota((rows, rows), 1) == source).astype(BF)


def vec_slots(rows):
    row, lane = iota((rows, CH), 0), iota((rows, CH), 1)
    return row, (row % SPAN == SPAN - 1) & (lane < VEC_LANES)


def back_matrix():
    row = iota((GROUP_ROWS, GROUP_ROWS), 0)
    column = iota((GROUP_ROWS, GROUP_ROWS), 1)
    source = (row // SPAN) % CUBOIDS * (GROUP * SPAN) + row // PEER_ROWS * SPAN + row % SPAN
    return (column == source).astype(BF)


def owner_kernel(
    recv_ref,
    vectors_ref,
    weights_ref,
    vup_ref,
    msg_ref,
    cells_ref,
    up_ref,
    delta_ref,
    query_m,
    grad_m,
    w_sum,
    g_sum,
    part_ref,
    low_ref,
    dkv_ref,
):
    group_tokens = GROUP * SPAN
    for u in range(CUBOIDS):
        cells_ref[u] = recv_ref[:, u].reshape(TOKENS, CH)
        up_ref[u] = recv_ref[:, CUBOIDS + u].reshape(TOKENS, CH)

    vectors = vectors_ref[...].astype(F32)
    w_q, w_k, w_v, w_o = (weights_ref[i] for i in range(4))
    w_kv = jnp.concatenate([w_k, w_v], axis=1)
    w_qkv = jnp.concatenate([w_q, w_kv], axis=1)
    w_q_t = w_q.T
    gk = head_blocks(global_rows(vectors, w_k))
    gv = head_blocks(global_rows(vectors, w_v))
    gk_b, gv_b = gk.astype(BF), gv.astype(BF)
    zero = jnp.zeros((PAIRS, CH), F32)
    shared = {}

    def global_operands():
        gq = head_blocks(global_rows(vectors, w_q))
        gg = head_blocks(global_upstream(vup_ref[...], w_o))
        gg3 = [part.astype(F32) for part in split3(gg)]
        shared["gq_b"] = gq.astype(BF)
        for name, blocks in (("gk_t", gk), ("gv_t", gv)):
            wide = jnp.concatenate([blocks, zero, zero, zero], axis=0)
            shared[name] = wide.T[:, :PAIRS].astype(BF)
        shared["gg_parts"] = jnp.concatenate(gg3, axis=0).astype(BF)
        shared["more"] = diagonal(
            jnp.concatenate([gq, gq, zero, zero], axis=0),
            jnp.concatenate([gg3[0], gg3[0], gg3[1], zero], axis=0),
        )

    def global_softmax():
        stats = recv_ref[:, 2 * CUBOIDS].astype(F32).reshape(PEERS * SPAN, CH)
        stats = stats + pltpu.roll(stats, CH - PAIRS, 1) + pltpu.roll(stats, CH - 2 * PAIRS, 1)
        stats = stats.reshape(PEERS, SPAN, CH)
        tops = stats[:, 0:1, :]
        top = jnp.max(tops, axis=0)
        summed = jnp.sum(jnp.exp(tops - top[None]) * stats, axis=0)
        lanes = jnp.where(iota((SPAN, CH), 0) == 0, top, summed)
        columns = jnp.concatenate([lanes, jnp.zeros((CH - SPAN, CH), F32)], axis=0).T
        shared["g_top"] = columns[:PAIRS, 0:1]
        shared["g_inv"] = 1.0 / columns[:PAIRS, 1:2]
        shared["g_row"] = columns[:PAIRS, 2:3] * shared["g_inv"]

    def clear(slot):
        query_m[slot] = jnp.zeros(query_m.shape[1:], BF)
        grad_m[slot] = jnp.zeros(grad_m.shape[1:], BF)

    clear(0)

    def heads(h):
        return slice(h * HDIM, (h + 1) * HDIM)

    class Cuboid:
        def __init__(self, u):
            self.u, self.slot = u, u % 2
            self.low = []
            self.rows = {n: [[] for _ in range(HEADS)] for n in ("p", "ds", "out", "dq")}

        def project_query(self):
            cells = cells_ref[self.u]
            self.query_t = dot_nt(w_q_t, cells).astype(BF)
            for h in range(HEADS):
                query_m[self.slot, h, heads(h), :] = self.query_t[heads(h)]

        def project_grad(self):
            self.grad_t = dot_nt(w_o, up_ref[self.u]).astype(BF)
            for h in range(HEADS):
                grad_m[self.slot, h, heads(h), :] = self.grad_t[heads(h)]

        def project_keys(self):
            self.key_value = dot(cells_ref[self.u], w_kv).astype(BF)
            self.key, self.value = self.key_value[:, :CH], self.key_value[:, CH:]

        def project_global(self):
            self.s_global = dot(gk_b, self.query_t)
            self.d_global = dot(gv_b, self.grad_t)

        def project_transposed(self):
            self.key_t = self.key.T
            self.value_t = self.value.T

        def project_rows(self):
            self.query = self.query_t.T
            self.grad = self.grad_t.T

        def scores(self, h, q):
            columns = pl.ds(q, QUERIES)
            return (
                dot(self.key, query_m[self.slot, h, :, columns]),
                dot(self.value, grad_m[self.slot, h, :, columns]),
            )

        def softmax(self, h, q, score, dprob):
            rows = slice(h * GLOBALS, (h + 1) * GLOBALS)
            s_glob = self.s_global[rows, q : q + QUERIES]
            d_glob = self.d_global[rows, q : q + QUERIES]
            top = jnp.maximum(
                jnp.max(score, axis=0, keepdims=True), jnp.max(s_glob, axis=0, keepdims=True)
            )
            e_local = jnp.exp2((score - top) * (SCALE * LOG2E))
            e_global = jnp.exp2((s_glob - top) * (SCALE * LOG2E))
            total = jnp.sum(e_local, axis=0, keepdims=True) + jnp.sum(
                e_global, axis=0, keepdims=True
            )
            inv = 1.0 / total
            p_local = e_local * inv
            p_global = e_global * inv
            inner = jnp.sum(p_local * dprob, axis=0, keepdims=True) + jnp.sum(
                p_global * d_glob, axis=0, keepdims=True
            )
            self.rows["p"][h].append(p_global)
            self.rows["ds"][h].append(p_global * (d_glob - inner) * SCALE)
            return p_local.astype(BF), (p_local * (dprob - inner) * SCALE).astype(BF)

        def products(self, h, q, p_low, ds_low):
            part = heads(h)
            self.rows["out"][h].append(dot(self.value_t[part], p_low))
            self.rows["dq"][h].append(dot(self.key_t[part], ds_low))
            self.low.append((p_low, ds_low))
            if q + QUERIES == TOKENS:
                p_low, ds_low = (jnp.concatenate(x, axis=1) for x in zip(*self.low))
                self.low = []
                dkv_ref[self.slot, :, part] = dot(ds_low, self.query)[:, part]
                lanes = slice(CH + part.start, CH + part.stop)
                dkv_ref[self.slot, :, lanes] = dot(p_low, self.grad)[:, part]

        def add(self, ref, where, value):
            ref[where] = value if self.u == 0 else ref[where] + value

        def whole(self, name):
            rows = [jnp.concatenate(row, axis=1) for row in self.rows[name]]
            return jnp.concatenate(rows, axis=0)

        def finish_queries(self):
            p_rows, ds_rows = self.whole("p").astype(BF), self.whole("ds").astype(BF)
            self.out_t = (self.whole("out") + dot(shared["gv_t"], p_rows)).astype(BF)
            self.dq_t = (self.whole("dq") + dot(shared["gk_t"], ds_rows)).astype(BF)
            rows = jnp.concatenate([ds_rows, p_rows], axis=0)
            g_both = dot(rows, jnp.concatenate([self.query, self.grad], axis=1))
            self.add(g_sum, 1, g_both[:PAIRS, :CH])
            self.add(g_sum, 2, g_both[PAIRS:, CH:])

        def finish_global(self):
            score = dot(shared["gq_b"], self.key_t) * SCALE
            prob = jnp.exp(score - shared["g_top"]) * shared["g_inv"]
            dprob = dot(shared["gg_parts"], self.value_t)
            dprob = dprob[:PAIRS] + dprob[PAIRS : 2 * PAIRS] + dprob[2 * PAIRS :]
            dscore = prob * (dprob - shared["g_row"]) * SCALE
            p_hi, p_mid, _ = split3(prob)
            d_hi, d_mid, _ = split3(dscore)
            none = jnp.zeros((PAIRS, TOKENS), BF)
            self.parts = jnp.concatenate(
                [d_hi, d_mid, none, none, p_hi, p_mid, p_hi, none], axis=0
            )
            g_both = dot(
                jnp.concatenate([d_hi, d_mid, p_hi, p_mid], axis=0), self.key_value
            )
            self.add(g_sum, 0, g_both[:PAIRS, :CH] + g_both[PAIRS : 2 * PAIRS, :CH])
            self.add(g_sum, 3, g_both[2 * PAIRS : 3 * PAIRS, CH:] + g_both[3 * PAIRS :, CH:])

        def finish_keys(self):
            more = dot(self.parts.T, shared["more"])
            self.d_key_value = (dkv_ref[self.slot] + more).astype(BF)

        def finish_weights(self):
            self.grads = jnp.concatenate([self.dq_t.T, self.d_key_value], axis=1)
            everything = slice(None)
            first, last = slice(0, 3 * CH), slice(3 * CH, 4 * CH)
            self.add(w_sum, (everything, first), dot(cells_ref[self.u].T, self.grads))
            self.add(w_sum, (everything, last), dot(self.out_t, up_ref[self.u]))

        def finish_cells(self):
            delta_ref[self.u] = dot_nt(self.grads, w_qkv).astype(BF)

        def before(self):
            return [
                self.project_query,
                self.project_grad,
                self.project_keys,
                self.project_global,
                self.project_transposed,
                self.project_rows,
            ]

        def after(self):
            return [
                self.finish_queries,
                self.finish_global,
                self.finish_keys,
                self.finish_weights,
                self.finish_cells,
            ]

    cuboids = [Cuboid(u) for u in range(CUBOIDS)]
    for task in cuboids[0].before():
        task()
    order = [(c, h, q) for c in cuboids for h in range(HEADS) for q in range(0, TOKENS, QUERIES)]
    per_cuboid = len(order) // CUBOIDS
    ready = cuboids[0].scores(*order[0][1:])
    low = None
    for i, (cuboid, *step) in enumerate(order):
        place = i % per_cuboid
        u = cuboid.u
        if place == 0:
            early = cuboids[u + 1].before() if u + 1 < CUBOIDS else []
            if u == 0:
                early.insert(0, lambda: clear(1))
            late = cuboids[u - 1].after() if u > 0 else [global_operands, global_softmax]
        following = None
        if place + 1 == per_cuboid:
            for task in early + late:
                task()
        if i + 1 < len(order):
            following = order[i + 1][0].scores(*order[i + 1][1:])
        now = cuboid.softmax(*step, *ready)
        if low is not None:
            order[i - 1][0].products(*order[i - 1][1:], *low)
        if place > 0 and late:
            late.pop(0)()
        low = now
        if early:
            early.pop(0)()
        ready = following
    order[-1][0].products(*order[-1][1:], *low)
    for task in cuboids[-1].after():
        task()

    def tall(pieces):
        rows = jnp.concatenate(pieces, axis=0)
        return jnp.concatenate([rows, jnp.zeros((CH - rows.shape[0], CH), F32)], axis=0)

    def parts_of(rows):
        return [part.astype(F32) for part in split3(rows)]

    g_parts = [parts_of(head_diagonal(g_sum[i])) for i in range(3)]
    g_tall = jnp.concatenate([tall(parts) for parts in g_parts], axis=1).astype(BF)
    w_sum[:, : 3 * CH] += dot(tall([vectors] * 3).T.astype(BF), g_tall)
    a_hi, a_mid, a_low = parts_of(head_diagonal(g_sum[3]))
    u_hi, u_mid, u_low = parts_of(vup_ref[...])
    left = tall([a_hi, a_hi, a_hi, a_mid, a_mid, a_low]).T.astype(BF)
    w_sum[:, 3 * CH :] += dot(left, tall([u_hi, u_mid, u_low, u_hi, u_mid, u_hi]).astype(BF))
    vec = dot_nt(g_tall[: 4 * GLOBALS], w_qkv)
    vec = vec[:GLOBALS] + vec[GLOBALS : 2 * GLOBALS] + vec[2 * GLOBALS : 3 * GLOBALS]
    for i in range(4):
        total = w_sum[:, i * CH : (i + 1) * CH]
        high = total.astype(BF)
        rows = pl.ds(i * CH, CH)
        part_ref[0, rows, :] = high
        low_ref[rows, :] = total - high.astype(F32)
    hi, mid, _ = split3(vec)
    vec_parts = jnp.concatenate(
        [hi.astype(F32), mid.astype(F32), jnp.zeros((CH - VEC_LANES, CH), F32)], axis=0
    ).T.astype(BF)
    row, slots = vec_slots(TOKENS)
    spread = (iota((TOKENS, CH), 0) // SPAN == iota((TOKENS, CH), 1)).astype(BF)
    part_ref[1] = jnp.where(slots, dot(spread, vec_parts), low_ref[...]).astype(BF)

    back = back_matrix()
    for i in range(PEERS // GROUP):
        tokens = pl.ds(i * group_tokens, group_tokens)
        rows = jnp.concatenate([delta_ref[u, tokens, :] for u in range(CUBOIDS)], axis=0)
        moved = dot(back, rows).astype(BF)
        msg_ref[pl.ds(i * GROUP, GROUP), 0:PEER_ROWS, :] = moved.reshape(GROUP, PEER_ROWS, CH)
    back = piece_matrix()
    for i in range(PEERS // PIECE_GROUP):
        tokens = pl.ds(i * CH, CH)
        rows = jnp.concatenate([part_ref[0, tokens, :], part_ref[1, tokens, :]], axis=0)
        moved = dot(back, rows).astype(BF)
        msg_ref[pl.ds(i * PIECE_GROUP, PIECE_GROUP), PEER_ROWS:, :] = moved.reshape(
            PIECE_GROUP, PIECE_ROWS, CH
        )


def sum_kernel(recv_ref, piece_ref):
    summed = jnp.sum(recv_ref[:, PEER_ROWS:, :].astype(F32), axis=0)
    row, slots = vec_slots(PIECE_ROWS)
    slots = slots & (row >= SPAN)
    vec = summed + pltpu.roll(summed, CH - GLOBALS, 1)
    low = jnp.where(slots, 0.0, summed)
    weight = summed[:SPAN] + low[SPAN:]
    high = weight.astype(BF).astype(F32)
    vec_high = vec.astype(BF).astype(F32)
    vec_low = pltpu.roll(vec - vec_high, GLOBALS, 1)
    vec = jnp.where(iota((PIECE_ROWS, CH), 1) < GLOBALS, vec_high, vec_low)
    piece = jnp.where(slots, vec, jnp.concatenate([high, weight - high], axis=0)).astype(BF)
    piece_ref[...] = jnp.broadcast_to(piece[None], piece_ref.shape)


def spread_kernel(recv_ref, weight_ref, vec_ref):
    rows = PIECE_GROUP * PIECE_ROWS
    row, slots = vec_slots(rows)
    slots = slots & (row % PIECE_ROWS >= SPAN)
    target, source = iota((CH, rows), 0), iota((CH, rows), 1)
    joins = (source // PIECE_ROWS == target // SPAN) & (source % SPAN == target % SPAN)
    joins = joins.astype(BF)
    target, source = iota((PIECE_GROUP, rows), 0), iota((PIECE_GROUP, rows), 1)
    last = (source == target * PIECE_ROWS + PIECE_ROWS - 1).astype(BF)
    vec = []
    for i in range(PEERS // PIECE_GROUP):
        piece = recv_ref[pl.ds(i * PIECE_GROUP, PIECE_GROUP)].reshape(rows, CH)
        vec.append(dot(last, piece))
        piece = jnp.where(slots, 0.0, piece.astype(F32)).astype(BF)
        weight_ref[i] = dot(joins, piece)
    vec = jnp.concatenate(vec, axis=0).T
    vec_ref[...] = vec[:GLOBALS] + vec[GLOBALS : 2 * GLOBALS]


def place_kernel(shift_hbm, recv_ref, out_ref, held, shift_ref, sem):
    copy = pltpu.make_async_copy(shift_hbm, shift_ref, sem)
    copy.start()
    for i in range(PEERS // GROUP):
        held[pl.ds(i * GROUP_ROWS, GROUP_ROWS), :] = recv_ref[
            pl.ds(i * GROUP, GROUP), 0:PEER_ROWS, :
        ].reshape(GROUP_ROWS, CH)
    held[CELLS_DEV:, :] = held[:WINDOW, :]
    copy.wait()
    offset = (CELLS_DEV - tile_offset(shift_ref)) % CELLS_DEV
    mover = shift_matrix(offset % 16, GROUP_ROWS, WINDOW)
    base = offset - offset % 16
    for i in range(CELLS_DEV // GROUP_ROWS):
        start = pl.multiple_of((base + i * GROUP_ROWS) % CELLS_DEV, 16)
        moved = dot(mover, held[pl.ds(start, WINDOW), :]).astype(BF)
        out_ref[pl.ds(i * GROUP_ROWS, GROUP_ROWS), :] = moved


VMEM = pl.BlockSpec(memory_space=pltpu.VMEM)
HBM = pl.BlockSpec(memory_space=pltpu.HBM)
PACK_PARAMS = pltpu.CompilerParams(vmem_limit_bytes=58_000_000)
PARAMS = pltpu.CompilerParams(vmem_limit_bytes=48 * 1024 * 1024)


def exchange(rows):
    return lax.all_to_all(rows, ("tile", "frame"), split_axis=0, concat_axis=0, tiled=True)


def body(cells, vectors, weights, cuboid_shift, cell_upstream, vector_upstream):
    message = pl.pallas_call(
        pack_kernel,
        out_shape=pltpu.VMEM((PEERS, MSG_SPANS, SPAN, CH), BF),
        in_specs=[HBM] * 6,
        out_specs=VMEM,
        scratch_shapes=[
            pltpu.VMEM((CELLS_DEV + WINDOW, 2 * CH), BF),
            pltpu.VMEM((GLOBALS, CH), BF),
            pltpu.VMEM((4, CH, CH), BF),
            pltpu.VMEM((GLOBALS, CH), F32),
            pltpu.SMEM((1,), jnp.int32),
            pltpu.SemaphoreType.DMA((8,)),
        ],
        compiler_params=PACK_PARAMS,
        name="pack",
    )(cuboid_shift, cells[0], cell_upstream[0], vectors, weights, vector_upstream)
    received = exchange(message)
    message = pl.pallas_call(
        owner_kernel,
        out_shape=pltpu.VMEM((PEERS, PEER_ROWS + PIECE_ROWS, CH), BF),
        in_specs=[VMEM] * 4,
        out_specs=VMEM,
        scratch_shapes=[
            pltpu.VMEM((CUBOIDS, TOKENS, CH), BF),
            pltpu.VMEM((CUBOIDS, TOKENS, CH), BF),
            pltpu.VMEM((CUBOIDS, TOKENS, CH), BF),
            pltpu.VMEM((2, HEADS, CH, TOKENS), BF),
            pltpu.VMEM((2, HEADS, CH, TOKENS), BF),
            pltpu.VMEM((CH, 4 * CH), F32),
            pltpu.VMEM((4, PAIRS, CH), F32),
            pltpu.VMEM((2, TOKENS, CH), BF),
            pltpu.VMEM((TOKENS, CH), F32),
            pltpu.VMEM((2, TOKENS, 2 * CH), F32),
        ],
        compiler_params=PARAMS,
        name="owner",
    )(received, vectors, weights, vector_upstream)
    received = exchange(message)
    pieces = pl.pallas_call(
        sum_kernel,
        out_shape=pltpu.VMEM((PEERS, PIECE_ROWS, CH), BF),
        in_specs=[VMEM],
        out_specs=VMEM,
        compiler_params=PARAMS,
        name="sum_pieces",
    )(received)
    pieces = exchange(pieces)
    cell_grad = pl.pallas_call(
        place_kernel,
        out_shape=jax.ShapeDtypeStruct((CELLS_DEV, CH), BF),
        in_specs=[HBM, VMEM],
        out_specs=VMEM,
        scratch_shapes=[
            pltpu.VMEM((CELLS_DEV + WINDOW, CH), BF),
            pltpu.SMEM((1,), jnp.int32),
            pltpu.SemaphoreType.DMA,
        ],
        compiler_params=PARAMS,
        name="place",
    )(cuboid_shift, received)
    weight_grad, vector_grad = pl.pallas_call(
        spread_kernel,
        out_shape=[
            jax.ShapeDtypeStruct((4, CH, CH), F32),
            jax.ShapeDtypeStruct((GLOBALS, CH), F32),
        ],
        in_specs=[VMEM],
        out_specs=[VMEM, VMEM],
        compiler_params=PARAMS,
        name="spread",
    )(pieces)
    return cell_grad[None], weight_grad, vector_grad


def solution(mesh):
    in_specs = (P("frame", "tile", None), P(), P(), P(), P("frame", "tile", None), P())
    out_specs = (P("frame", "tile", None), P(), P())
    return jax.shard_map(body, mesh=mesh, in_specs=in_specs, out_specs=out_specs, check_vma=False)
```

profile of v0, /device:TPU:1, one launch (start us, length us, event | category | flops | bytes accessed | tf_op | source)
XLA Modules:
  0.0 92.0 jit_solution(8179991975882116161)
XLA Ops:
  1.3 3.1 %pack.1 = bf16[128,9,4,128]{3,2,1,0:T(4,128)(2,1)S(1)} custom-call(s32[1]{0:T(128)S(6)} %copy.9.shift_hbm, bf16[2048,128]{1,0:T(8,128)(2,1)} %bitcast.4, bf16[2048,128]{1,0:T(8,128)(2,1)} %bitcast.5, bf16[8,128]{1,0:T(8,128)(2,1)} %vectors_ref.1, bf16[4,128,128]{2,1,0:T(8,128)(2,1)} %weights_ref.1, f32[8,128]{1,0:T(8,128)} %vup_ref.1), custom_call_target="tpu_custom_call" | custom-call | tf_op jit(solution)/shard_map/pack/pallas_call | solution.py:535
  4.3 0.0 copy-start
  4.3 0.0 copy-start.1
  4.4 0.0 copy-start.2
  4.4 32.1 %all_to_all.15.recv_ref = bf16[128,9,4,128]{3,2,1,0:T(4,128)(2,1)S(1)} all-to-all(bf16[128,9,4,128]{3,2,1,0:T(4,128)(2,1)S(1)} %pack.1), channel_id=1, replica_groups=mesh['tile'=32,'frame'=4] {'tile','frame'}, dimensions={0} | all-to-all | bytes 2359296 | tf_op jit(solution)/shard_map/all_to_all | solution.py:531
  36.5 0.0 copy-done
  36.5 0.0 copy-done.1
  36.5 0.0 copy-done.2
  36.5 18.1 %owner.1 = bf16[128,24,128]{2,1,0:T(8,128)(2,1)S(1)} custom-call(bf16[128,9,4,128]{3,2,1,0:T(4,128)(2,1)S(1)} %all_to_all.15.recv_ref, bf16[8,128]{1,0:T(8,128)(2,1)S(1)} %copy-done.2, bf16[4,128,128]{2,1,0:T(8,128)(2,1)S(1)} %copy-done, f32[8,128]{1,0:T(8,128)S(1)} %copy-done.1), custom_call_target="tpu_custom_call" | custom-call | tf_op jit(solution)/shard_map/owner/pallas_call | solution.py:552
  54.6 20.3 %all_to_all.16.recv_ref = bf16[128,24,128]{2,1,0:T(8,128)(2,1)S(1)} all-to-all(bf16[128,24,128]{2,1,0:T(8,128)(2,1)S(1)} %owner.1), channel_id=1, replica_groups=mesh['tile'=32,'frame'=4] {'tile','frame'}, dimensions={0} | all-to-all | bytes 1572864 | tf_op jit(solution)/shard_map/all_to_all | solution.py:531
  74.9 1.0 %sum_pieces.1 = bf16[128,8,128]{2,1,0:T(8,128)(2,1)} custom-call(bf16[128,24,128]{2,1,0:T(8,128)(2,1)S(1)} %all_to_all.16.recv_ref), custom_call_target="tpu_custom_call" | custom-call | tf_op jit(solution)/shard_map/sum_pieces/pallas_call | solution.py:573
  75.9 3.8 %all-to-all-start.2 = ((bf16[128,8,128]{2,1,0:T(8,128)(2,1)}), bf16[128,8,128]{2,1,0:T(8,128)(2,1)S(1)}, u32[]{:S(2)}, u32[]{:S(2)}) async-start(bf16[128,8,128]{2,1,0:T(8,128)(2,1)} %sum_pieces.1), calls=%async_computation.2 | async-start | bytes 524288 | tf_op jit(solution)/shard_map/all_to_all | solution.py:531
  79.7 1.9 %place.1 = bf16[2048,128]{1,0:T(8,128)(2,1)} custom-call(s32[1]{0:T(128)S(6)} %copy.9.shift_hbm, bf16[128,24,128]{2,1,0:T(8,128)(2,1)S(1)} %all_to_all.16.recv_ref), custom_call_target="tpu_custom_call" | custom-call | tf_op jit(solution)/shard_map/place/pallas_call | solution.py:582
  81.6 9.3 %all-to-all-done.2.recv_ref = bf16[128,8,128]{2,1,0:T(8,128)(2,1)S(1)} async-done(((bf16[128,8,128]{2,1,0:T(8,128)(2,1)}), bf16[128,8,128]{2,1,0:T(8,128)(2,1)S(1)}, u32[]{:S(2)}, u32[]{:S(2)}) %all-to-all-start.2) | async-done | bytes 262176 | tf_op jit(solution)/shard_map/all_to_all | solution.py:531
  90.9 1.0 %spread.1 = (f32[4,128,128]{2,1,0:T(8,128)}, f32[8,128]{1,0:T(8,128)}) custom-call(bf16[128,8,128]{2,1,0:T(8,128)(2,1)S(1)} %all-to-all-done.2.recv_ref), custom_call_target="tpu_custom_call" | custom-call | tf_op jit(solution)/shard_map/spread/pallas_call | solution.py:595
Async XLA Ops:
  4.3 32.1 %copy-start = (bf16[4,128,128]{2,1,0:T(8,128)(2,1)S(1)}, bf16[4,128,128]{2,1,0:T(8,128)(2,1)}, u32[]{:S(2)}) copy-start(bf16[4,128,128]{2,1,0:T(8,128)(2,1)} %weights_ref.1) | copy-start | bytes 393220
  4.3 32.1 %copy-start.1 = (f32[8,128]{1,0:T(8,128)S(1)}, f32[8,128]{1,0:T(8,128)}, u32[]{:S(2)}) copy-start(f32[8,128]{1,0:T(8,128)} %vup_ref.1) | copy-start | bytes 12292
  4.4 32.1 %copy-start.2 = (bf16[8,128]{1,0:T(8,128)(2,1)S(1)}, bf16[8,128]{1,0:T(8,128)(2,1)}, u32[]{:S(2)}) copy-start(bf16[8,128]{1,0:T(8,128)(2,1)} %vectors_ref.1) | copy-start | bytes 6148
  75.9 15.1 %all-to-all-start.2 = ((bf16[128,8,128]{2,1,0:T(8,128)(2,1)}), bf16[128,8,128]{2,1,0:T(8,128)(2,1)S(1)}, u32[]{:S(2)}, u32[]{:S(2)}) async-start(bf16[128,8,128]{2,1,0:T(8,128)(2,1)} %sum_pieces.1), calls=%async_computation.2 | async-start | bytes 524288 | tf_op jit(solution)/shard_map/all_to_all | solution.py:531
where the time goes:
time: 92.2 us; the launch traced here: 92 us
  blocking collectives  52.4 us (57%)
  Pallas kernels  25.1 us (27%)
  waiting for transfers between devices  9.33 us (10%)
  starting transfers between devices  3.81 us (4%)
  between operations  1.34 us (1%)
    all_to_all x2, blocking collectives, exchange(): lax.all_to_all(rows, ('tile', 'frame'), split_axis=0, concat_axis=0, tile...  52.4 us
    pallas_call x1, Pallas kernels, body(): pl.pallas_call(owner_kernel, out_shape=pltpu.VMEM((PEERS, PEER_ROWS + PIE...  18.1 us
    all_to_all x1, waiting for transfers between devices, exchange(): lax.all_to_all(rows, ('tile', 'frame'), split_axis=0, concat_axis=0, tile...  9.33 us
    all_to_all x1, starting transfers between devices, exchange(): lax.all_to_all(rows, ('tile', 'frame'), split_axis=0, concat_axis=0, tile...  3.81 us
    pallas_call x1, Pallas kernels, body(): pl.pallas_call(pack_kernel, out_shape=pltpu.VMEM((PEERS, MSG_SPANS, SPAN,...  3.05 us
    pallas_call x1, Pallas kernels, body(): pl.pallas_call(place_kernel, out_shape=jax.ShapeDtypeStruct((CELLS_DEV, C...  1.93 us
  transfers between devices with their start and end apart: 1, of which 1 were waited for; matrix products, arithmetic and copies ran while one was open for 0% of the time, Pallas kernels for 2%

commit v1 on v0

--- a/solution.py
+++ b/solution.py
@@ -197,10 +197,6 @@
     dkv_ref,
 ):
     group_tokens = GROUP * SPAN
-    for u in range(CUBOIDS):
-        cells_ref[u] = recv_ref[:, u].reshape(TOKENS, CH)
-        up_ref[u] = recv_ref[:, CUBOIDS + u].reshape(TOKENS, CH)
-
     vectors = vectors_ref[...].astype(F32)
     w_q, w_k, w_v, w_o = (weights_ref[i] for i in range(4))
     w_kv = jnp.concatenate([w_k, w_v], axis=1)
@@ -255,13 +251,16 @@
             self.rows = {n: [[] for _ in range(HEADS)] for n in ("p", "ds", "out", "dq")}
 
         def project_query(self):
-            cells = cells_ref[self.u]
+            cells = recv_ref[:, self.u].reshape(TOKENS, CH)
+            cells_ref[self.u] = cells
             self.query_t = dot_nt(w_q_t, cells).astype(BF)
             for h in range(HEADS):
                 query_m[self.slot, h, heads(h), :] = self.query_t[heads(h)]
 
         def project_grad(self):
-            self.grad_t = dot_nt(w_o, up_ref[self.u]).astype(BF)
+            upstream = recv_ref[:, CUBOIDS + self.u].reshape(TOKENS, CH)
+            up_ref[self.u] = upstream
+            self.grad_t = dot_nt(w_o, upstream).astype(BF)
             for h in range(HEADS):
                 grad_m[self.slot, h, heads(h), :] = self.grad_t[heads(h)]
 

time: 92.2 us -> 92.2 us (level)
  no operation moved by 1% of the time
where the time goes in v1:
time: 92.2 us; the launch traced here: 92 us
  blocking collectives  52.4 us (57%)
  Pallas kernels  25.1 us (27%)
  waiting for transfers between devices  9.33 us (10%)
  starting transfers between devices  3.81 us (4%)
  between operations  1.34 us (1%)
    all_to_all x2, blocking collectives, exchange(): lax.all_to_all(rows, ('tile', 'frame'), split_axis=0, concat_axis=0, tile...  52.4 us
    pallas_call x1, Pallas kernels, body(): pl.pallas_call(owner_kernel, out_shape=pltpu.VMEM((PEERS, PEER_ROWS + PIE...  18.1 us
    all_to_all x1, waiting for transfers between devices, exchange(): lax.all_to_all(rows, ('tile', 'frame'), split_axis=0, concat_axis=0, tile...  9.33 us
    all_to_all x1, starting transfers between devices, exchange(): lax.all_to_all(rows, ('tile', 'frame'), split_axis=0, concat_axis=0, tile...  3.81 us
    pallas_call x1, Pallas kernels, body(): pl.pallas_call(pack_kernel, out_shape=pltpu.VMEM((PEERS, MSG_SPANS, SPAN,...  3.05 us
    pallas_call x1, Pallas kernels, body(): pl.pallas_call(place_kernel, out_shape=jax.ShapeDtypeStruct((CELLS_DEV, C...  1.93 us
  transfers between devices with their start and end apart: 1, of which 1 were waited for; matrix products, arithmetic and copies ran while one was open for 0% of the time, Pallas kernels for 2%

profile of v1, /device:TPU:1, one launch (start us, length us, event | category | flops | bytes accessed | tf_op | source)
XLA Modules:
  0.0 92.0 jit_solution(6670187478249466110)
XLA Ops:
  1.3 3.1 %pack.1 = bf16[128,9,4,128]{3,2,1,0:T(4,128)(2,1)S(1)} custom-call(s32[1]{0:T(128)S(6)} %copy.9.shift_hbm, bf16[2048,128]{1,0:T(8,128)(2,1)} %bitcast.4, bf16[2048,128]{1,0:T(8,128)(2,1)} %bitcast.5, bf16[8,128]{1,0:T(8,128)(2,1)} %vectors_ref.1, bf16[4,128,128]{2,1,0:T(8,128)(2,1)} %weights_ref.1, f32[8,128]{1,0:T(8,128)} %vup_ref.1), custom_call_target="tpu_custom_call" | custom-call | tf_op jit(solution)/shard_map/pack/pallas_call | solution.py:534
  4.3 0.0 copy-start
  4.3 0.0 copy-start.1
  4.4 0.0 copy-start.2
  4.4 32.1 %all_to_all.15.recv_ref = bf16[128,9,4,128]{3,2,1,0:T(4,128)(2,1)S(1)} all-to-all(bf16[128,9,4,128]{3,2,1,0:T(4,128)(2,1)S(1)} %pack.1), channel_id=1, replica_groups=mesh['tile'=32,'frame'=4] {'tile','frame'}, dimensions={0} | all-to-all | bytes 2359296 | tf_op jit(solution)/shard_map/all_to_all | solution.py:530
  36.5 0.0 copy-done
  36.5 0.0 copy-done.1
  36.5 0.0 copy-done.2
  36.5 18.1 %owner.1 = bf16[128,24,128]{2,1,0:T(8,128)(2,1)S(1)} custom-call(bf16[128,9,4,128]{3,2,1,0:T(4,128)(2,1)S(1)} %all_to_all.15.recv_ref, bf16[8,128]{1,0:T(8,128)(2,1)S(1)} %copy-done.2, bf16[4,128,128]{2,1,0:T(8,128)(2,1)S(1)} %copy-done, f32[8,128]{1,0:T(8,128)S(1)} %copy-done.1), custom_call_target="tpu_custom_call" | custom-call | tf_op jit(solution)/shard_map/owner/pallas_call | solution.py:551
  54.6 20.3 %all_to_all.16.recv_ref = bf16[128,24,128]{2,1,0:T(8,128)(2,1)S(1)} all-to-all(bf16[128,24,128]{2,1,0:T(8,128)(2,1)S(1)} %owner.1), channel_id=1, replica_groups=mesh['tile'=32,'frame'=4] {'tile','frame'}, dimensions={0} | all-to-all | bytes 1572864 | tf_op jit(solution)/shard_map/all_to_all | solution.py:530
  74.9 1.0 %sum_pieces.1 = bf16[128,8,128]{2,1,0:T(8,128)(2,1)} custom-call(bf16[128,24,128]{2,1,0:T(8,128)(2,1)S(1)} %all_to_all.16.recv_ref), custom_call_target="tpu_custom_call" | custom-call | tf_op jit(solution)/shard_map/sum_pieces/pallas_call | solution.py:572
  75.9 3.8 %all-to-all-start.2 = ((bf16[128,8,128]{2,1,0:T(8,128)(2,1)}), bf16[128,8,128]{2,1,0:T(8,128)(2,1)S(1)}, u32[]{:S(2)}, u32[]{:S(2)}) async-start(bf16[128,8,128]{2,1,0:T(8,128)(2,1)} %sum_pieces.1), calls=%async_computation.2 | async-start | bytes 524288 | tf_op jit(solution)/shard_map/all_to_all | solution.py:530
  79.7 1.9 %place.1 = bf16[2048,128]{1,0:T(8,128)(2,1)} custom-call(s32[1]{0:T(128)S(6)} %copy.9.shift_hbm, bf16[128,24,128]{2,1,0:T(8,128)(2,1)S(1)} %all_to_all.16.recv_ref), custom_call_target="tpu_custom_call" | custom-call | tf_op jit(solution)/shard_map/place/pallas_call | solution.py:581
  81.6 9.3 %all-to-all-done.2.recv_ref = bf16[128,8,128]{2,1,0:T(8,128)(2,1)S(1)} async-done(((bf16[128,8,128]{2,1,0:T(8,128)(2,1)}), bf16[128,8,128]{2,1,0:T(8,128)(2,1)S(1)}, u32[]{:S(2)}, u32[]{:S(2)}) %all-to-all-start.2) | async-done | bytes 262176 | tf_op jit(solution)/shard_map/all_to_all | solution.py:530
  91.0 1.0 %spread.1 = (f32[4,128,128]{2,1,0:T(8,128)}, f32[8,128]{1,0:T(8,128)}) custom-call(bf16[128,8,128]{2,1,0:T(8,128)(2,1)S(1)} %all-to-all-done.2.recv_ref), custom_call_target="tpu_custom_call" | custom-call | tf_op jit(solution)/shard_map/spread/pallas_call | solution.py:594
Async XLA Ops:
  4.3 32.1 %copy-start = (bf16[4,128,128]{2,1,0:T(8,128)(2,1)S(1)}, bf16[4,128,128]{2,1,0:T(8,128)(2,1)}, u32[]{:S(2)}) copy-start(bf16[4,128,128]{2,1,0:T(8,128)(2,1)} %weights_ref.1) | copy-start | bytes 393220
  4.3 32.1 %copy-start.1 = (f32[8,128]{1,0:T(8,128)S(1)}, f32[8,128]{1,0:T(8,128)}, u32[]{:S(2)}) copy-start(f32[8,128]{1,0:T(8,128)} %vup_ref.1) | copy-start | bytes 12292
  4.4 32.1 %copy-start.2 = (bf16[8,128]{1,0:T(8,128)(2,1)S(1)}, bf16[8,128]{1,0:T(8,128)(2,1)}, u32[]{:S(2)}) copy-start(bf16[8,128]{1,0:T(8,128)(2,1)} %vectors_ref.1) | copy-start | bytes 6148
  75.9 15.1 %all-to-all-start.2 = ((bf16[128,8,128]{2,1,0:T(8,128)(2,1)}), bf16[128,8,128]{2,1,0:T(8,128)(2,1)S(1)}, u32[]{:S(2)}, u32[]{:S(2)}) async-start(bf16[128,8,128]{2,1,0:T(8,128)(2,1)} %sum_pieces.1), calls=%async_computation.2 | async-start | bytes 524288 | tf_op jit(solution)/shard_map/all_to_all | solution.py:530

commit v2 on v1

--- a/solution.py
+++ b/solution.py
@@ -160,23 +160,9 @@
         msg_ref[peers, CUBOIDS : 2 * CUBOIDS] = moved[:, CH:].reshape(shape)
 
 
-def piece_matrix():
-    rows = PIECE_GROUP * PIECE_ROWS
-    row = iota((rows, rows), 0)
-    source = row // SPAN % 2 * CH + row // PIECE_ROWS * SPAN + row % SPAN
-    return (iota((rows, rows), 1) == source).astype(BF)
-
-
 def vec_slots(rows):
     row, lane = iota((rows, CH), 0), iota((rows, CH), 1)
     return row, (row % SPAN == SPAN - 1) & (lane < VEC_LANES)
-
-
-def back_matrix():
-    row = iota((GROUP_ROWS, GROUP_ROWS), 0)
-    column = iota((GROUP_ROWS, GROUP_ROWS), 1)
-    source = (row // SPAN) % CUBOIDS * (GROUP * SPAN) + row // PEER_ROWS * SPAN + row % SPAN
-    return (column == source).astype(BF)
 
 
 def owner_kernel(
@@ -187,16 +173,13 @@
     msg_ref,
     cells_ref,
     up_ref,
-    delta_ref,
     query_m,
     grad_m,
     w_sum,
     g_sum,
-    part_ref,
     low_ref,
     dkv_ref,
 ):
-    group_tokens = GROUP * SPAN
     vectors = vectors_ref[...].astype(F32)
     w_q, w_k, w_v, w_o = (weights_ref[i] for i in range(4))
     w_kv = jnp.concatenate([w_k, w_v], axis=1)
@@ -367,7 +350,8 @@
             self.add(w_sum, (everything, last), dot(self.out_t, up_ref[self.u]))
 
         def finish_cells(self):
-            delta_ref[self.u] = dot_nt(self.grads, w_qkv).astype(BF)
+            delta = dot_nt(self.grads, w_qkv).astype(BF)
+            msg_ref[:, self.u] = delta.reshape(PEERS, SPAN, CH)
 
         def before(self):
             return [
@@ -441,35 +425,22 @@
     for i in range(4):
         total = w_sum[:, i * CH : (i + 1) * CH]
         high = total.astype(BF)
-        rows = pl.ds(i * CH, CH)
-        part_ref[0, rows, :] = high
-        low_ref[rows, :] = total - high.astype(F32)
+        peers = pl.ds(i * PIECE_GROUP, PIECE_GROUP)
+        msg_ref[peers, CUBOIDS] = high.reshape(PIECE_GROUP, SPAN, CH)
+        low_ref[pl.ds(i * CH, CH), :] = total - high.astype(F32)
     hi, mid, _ = split3(vec)
     vec_parts = jnp.concatenate(
         [hi.astype(F32), mid.astype(F32), jnp.zeros((CH - VEC_LANES, CH), F32)], axis=0
     ).T.astype(BF)
     row, slots = vec_slots(TOKENS)
     spread = (iota((TOKENS, CH), 0) // SPAN == iota((TOKENS, CH), 1)).astype(BF)
-    part_ref[1] = jnp.where(slots, dot(spread, vec_parts), low_ref[...]).astype(BF)
-
-    back = back_matrix()
-    for i in range(PEERS // GROUP):
-        tokens = pl.ds(i * group_tokens, group_tokens)
-        rows = jnp.concatenate([delta_ref[u, tokens, :] for u in range(CUBOIDS)], axis=0)
-        moved = dot(back, rows).astype(BF)
-        msg_ref[pl.ds(i * GROUP, GROUP), 0:PEER_ROWS, :] = moved.reshape(GROUP, PEER_ROWS, CH)
-    back = piece_matrix()
-    for i in range(PEERS // PIECE_GROUP):
-        tokens = pl.ds(i * CH, CH)
-        rows = jnp.concatenate([part_ref[0, tokens, :], part_ref[1, tokens, :]], axis=0)
-        moved = dot(back, rows).astype(BF)
-        msg_ref[pl.ds(i * PIECE_GROUP, PIECE_GROUP), PEER_ROWS:, :] = moved.reshape(
-            PIECE_GROUP, PIECE_ROWS, CH
-        )
+    low_rows = jnp.where(slots, dot(spread, vec_parts), low_ref[...]).astype(BF)
+    msg_ref[:, CUBOIDS + 1] = low_rows.reshape(PEERS, SPAN, CH)
 
 
 def sum_kernel(recv_ref, piece_ref):
-    summed = jnp.sum(recv_ref[:, PEER_ROWS:, :].astype(F32), axis=0)
+    summed = jnp.sum(recv_ref[:, CUBOIDS:].astype(F32), axis=0)
+    summed = jnp.concatenate([summed[0], summed[1]], axis=0)
     row, slots = vec_slots(PIECE_ROWS)
     slots = slots & (row >= SPAN)
     vec = summed + pltpu.roll(summed, CH - GLOBALS, 1)
@@ -479,26 +450,20 @@
     vec_high = vec.astype(BF).astype(F32)
     vec_low = pltpu.roll(vec - vec_high, GLOBALS, 1)
     vec = jnp.where(iota((PIECE_ROWS, CH), 1) < GLOBALS, vec_high, vec_low)
-    piece = jnp.where(slots, vec, jnp.concatenate([high, weight - high], axis=0)).astype(BF)
-    piece_ref[...] = jnp.broadcast_to(piece[None], piece_ref.shape)
+    piece = jnp.where(slots, vec, jnp.concatenate([high, weight - high], axis=0))
+    for i in range(2):
+        rows = piece[i * SPAN : (i + 1) * SPAN].astype(BF)
+        piece_ref[:, i] = jnp.broadcast_to(rows[None], (PEERS, SPAN, CH))
 
 
 def spread_kernel(recv_ref, weight_ref, vec_ref):
-    rows = PIECE_GROUP * PIECE_ROWS
-    row, slots = vec_slots(rows)
-    slots = slots & (row % PIECE_ROWS >= SPAN)
-    target, source = iota((CH, rows), 0), iota((CH, rows), 1)
-    joins = (source // PIECE_ROWS == target // SPAN) & (source % SPAN == target % SPAN)
-    joins = joins.astype(BF)
-    target, source = iota((PIECE_GROUP, rows), 0), iota((PIECE_GROUP, rows), 1)
-    last = (source == target * PIECE_ROWS + PIECE_ROWS - 1).astype(BF)
-    vec = []
-    for i in range(PEERS // PIECE_GROUP):
-        piece = recv_ref[pl.ds(i * PIECE_GROUP, PIECE_GROUP)].reshape(rows, CH)
-        vec.append(dot(last, piece))
-        piece = jnp.where(slots, 0.0, piece.astype(F32)).astype(BF)
-        weight_ref[i] = dot(joins, piece)
-    vec = jnp.concatenate(vec, axis=0).T
+    high = recv_ref[:, 0].reshape(TOKENS, CH)
+    low = recv_ref[:, 1].reshape(TOKENS, CH)
+    _, slots = vec_slots(TOKENS)
+    weight = high.astype(F32) + jnp.where(slots, 0.0, low.astype(F32))
+    weight_ref[...] = weight.reshape(4, CH, CH)
+    target, source = iota((PEERS, TOKENS), 0), iota((PEERS, TOKENS), 1)
+    vec = dot((source == target * SPAN + SPAN - 1).astype(BF), low).T
     vec_ref[...] = vec[:GLOBALS] + vec[GLOBALS : 2 * GLOBALS]
 
 
@@ -507,7 +472,7 @@
     copy.start()
     for i in range(PEERS // GROUP):
         held[pl.ds(i * GROUP_ROWS, GROUP_ROWS), :] = recv_ref[
-            pl.ds(i * GROUP, GROUP), 0:PEER_ROWS, :
+            pl.ds(i * GROUP, GROUP), 0:CUBOIDS
         ].reshape(GROUP_ROWS, CH)
     held[CELLS_DEV:, :] = held[:WINDOW, :]
     copy.wait()
@@ -550,18 +515,16 @@
     received = exchange(message)
     message = pl.pallas_call(
         owner_kernel,
-        out_shape=pltpu.VMEM((PEERS, PEER_ROWS + PIECE_ROWS, CH), BF),
+        out_shape=pltpu.VMEM((PEERS, CUBOIDS + 2, SPAN, CH), BF),
         in_specs=[VMEM] * 4,
         out_specs=VMEM,
         scratch_shapes=[
-            pltpu.VMEM((CUBOIDS, TOKENS, CH), BF),
             pltpu.VMEM((CUBOIDS, TOKENS, CH), BF),
             pltpu.VMEM((CUBOIDS, TOKENS, CH), BF),
             pltpu.VMEM((2, HEADS, CH, TOKENS), BF),
             pltpu.VMEM((2, HEADS, CH, TOKENS), BF),
             pltpu.VMEM((CH, 4 * CH), F32),
             pltpu.VMEM((4, PAIRS, CH), F32),
-            pltpu.VMEM((2, TOKENS, CH), BF),
             pltpu.VMEM((TOKENS, CH), F32),
             pltpu.VMEM((2, TOKENS, 2 * CH), F32),
         ],
@@ -571,7 +534,7 @@
     received = exchange(message)
     pieces = pl.pallas_call(
         sum_kernel,
-        out_shape=pltpu.VMEM((PEERS, PIECE_ROWS, CH), BF),
+        out_shape=pltpu.VMEM((PEERS, 2, SPAN, CH), BF),
         in_specs=[VMEM],
         out_specs=VMEM,
         compiler_params=PARAMS,

time: 92.2 us -> 91.6 us (level)
  no operation moved by 1% of the time
where the time goes in v2:
time: 91.6 us; the launch traced here: 91.4 us
  blocking collectives  52.4 us (57%)
  Pallas kernels  24.5 us (27%)
  waiting for transfers between devices  9.33 us (10%)
  starting transfers between devices  3.81 us (4%)
  between operations  1.34 us (1%)
    all_to_all x2, blocking collectives, exchange(): lax.all_to_all(rows, ('tile', 'frame'), split_axis=0, concat_axis=0, tile...  52.4 us
    pallas_call x1, Pallas kernels, body(): pl.pallas_call(owner_kernel, out_shape=pltpu.VMEM((PEERS, CUBOIDS + 2, SP...  17.5 us
    all_to_all x1, waiting for transfers between devices, exchange(): lax.all_to_all(rows, ('tile', 'frame'), split_axis=0, concat_axis=0, tile...  9.33 us
    all_to_all x1, starting transfers between devices, exchange(): lax.all_to_all(rows, ('tile', 'frame'), split_axis=0, concat_axis=0, tile...  3.81 us
    pallas_call x1, Pallas kernels, body(): pl.pallas_call(pack_kernel, out_shape=pltpu.VMEM((PEERS, MSG_SPANS, SPAN,...  3.05 us
    pallas_call x1, Pallas kernels, body(): pl.pallas_call(place_kernel, out_shape=jax.ShapeDtypeStruct((CELLS_DEV, C...  1.93 us
  transfers between devices with their start and end apart: 1, of which 1 were waited for; matrix products, arithmetic and copies ran while one was open for 0% of the time, Pallas kernels for 2%

profile of v2, /device:TPU:1, one launch (start us, length us, event | category | flops | bytes accessed | tf_op | source)
XLA Modules:
  0.0 91.4 jit_solution(16578738609638380208)
XLA Ops:
  1.3 3.1 %pack.1 = bf16[128,9,4,128]{3,2,1,0:T(4,128)(2,1)S(1)} custom-call(s32[1]{0:T(128)S(6)} %copy.9.shift_hbm, bf16[2048,128]{1,0:T(8,128)(2,1)} %bitcast.4, bf16[2048,128]{1,0:T(8,128)(2,1)} %bitcast.5, bf16[8,128]{1,0:T(8,128)(2,1)} %vectors_ref.1, bf16[4,128,128]{2,1,0:T(8,128)(2,1)} %weights_ref.1, f32[8,128]{1,0:T(8,128)} %vup_ref.1), custom_call_target="tpu_custom_call" | custom-call | tf_op jit(solution)/shard_map/pack/pallas_call | solution.py:499
  4.3 0.0 copy-start
  4.3 0.0 copy-start.1
  4.4 0.0 copy-start.2
  4.4 32.1 %all_to_all.15.recv_ref = bf16[128,9,4,128]{3,2,1,0:T(4,128)(2,1)S(1)} all-to-all(bf16[128,9,4,128]{3,2,1,0:T(4,128)(2,1)S(1)} %pack.1), channel_id=1, replica_groups=mesh['tile'=32,'frame'=4] {'tile','frame'}, dimensions={0} | all-to-all | bytes 2359296 | tf_op jit(solution)/shard_map/all_to_all | solution.py:495
  36.5 0.0 copy-done
  36.5 0.0 copy-done.1
  36.5 0.0 copy-done.2
  36.5 17.5 %owner.1 = bf16[128,6,4,128]{3,2,1,0:T(4,128)(2,1)S(1)} custom-call(bf16[128,9,4,128]{3,2,1,0:T(4,128)(2,1)S(1)} %all_to_all.15.recv_ref, bf16[8,128]{1,0:T(8,128)(2,1)S(1)} %copy-done.2, bf16[4,128,128]{2,1,0:T(8,128)(2,1)S(1)} %copy-done, f32[8,128]{1,0:T(8,128)S(1)} %copy-done.1), custom_call_target="tpu_custom_call" | custom-call | tf_op jit(solution)/shard_map/owner/pallas_call | solution.py:516
  54.0 20.3 %all_to_all.16.recv_ref = bf16[128,6,4,128]{3,2,1,0:T(4,128)(2,1)S(1)} all-to-all(bf16[128,6,4,128]{3,2,1,0:T(4,128)(2,1)S(1)} %owner.1), channel_id=1, replica_groups=mesh['tile'=32,'frame'=4] {'tile','frame'}, dimensions={0} | all-to-all | bytes 1572864 | tf_op jit(solution)/shard_map/all_to_all | solution.py:495
  74.3 1.1 %sum_pieces.1 = bf16[128,2,4,128]{3,2,1,0:T(4,128)(2,1)} custom-call(bf16[128,6,4,128]{3,2,1,0:T(4,128)(2,1)S(1)} %all_to_all.16.recv_ref), custom_call_target="tpu_custom_call" | custom-call | tf_op jit(solution)/shard_map/sum_pieces/pallas_call | solution.py:535
  75.4 3.8 %all-to-all-start.2 = ((bf16[128,2,4,128]{3,2,1,0:T(4,128)(2,1)}), bf16[128,2,4,128]{3,2,1,0:T(4,128)(2,1)S(1)}, u32[]{:S(2)}, u32[]{:S(2)}) async-start(bf16[128,2,4,128]{3,2,1,0:T(4,128)(2,1)} %sum_pieces.1), calls=%async_computation.2 | async-start | bytes 524288 | tf_op jit(solution)/shard_map/all_to_all | solution.py:495
  79.2 1.9 %place.1 = bf16[2048,128]{1,0:T(8,128)(2,1)} custom-call(s32[1]{0:T(128)S(6)} %copy.9.shift_hbm, bf16[128,6,4,128]{3,2,1,0:T(4,128)(2,1)S(1)} %all_to_all.16.recv_ref), custom_call_target="tpu_custom_call" | custom-call | tf_op jit(solution)/shard_map/place/pallas_call | solution.py:544
  81.1 9.3 %all-to-all-done.2.recv_ref = bf16[128,2,4,128]{3,2,1,0:T(4,128)(2,1)S(1)} async-done(((bf16[128,2,4,128]{3,2,1,0:T(4,128)(2,1)}), bf16[128,2,4,128]{3,2,1,0:T(4,128)(2,1)S(1)}, u32[]{:S(2)}, u32[]{:S(2)}) %all-to-all-start.2) | async-done | bytes 262176 | tf_op jit(solution)/shard_map/all_to_all | solution.py:495
  90.4 0.9 %spread.1 = (f32[4,128,128]{2,1,0:T(8,128)}, f32[8,128]{1,0:T(8,128)}) custom-call(bf16[128,2,4,128]{3,2,1,0:T(4,128)(2,1)S(1)} %all-to-all-done.2.recv_ref), custom_call_target="tpu_custom_call" | custom-call | tf_op jit(solution)/shard_map/spread/pallas_call | solution.py:557
Async XLA Ops:
  4.3 32.1 %copy-start = (bf16[4,128,128]{2,1,0:T(8,128)(2,1)S(1)}, bf16[4,128,128]{2,1,0:T(8,128)(2,1)}, u32[]{:S(2)}) copy-start(bf16[4,128,128]{2,1,0:T(8,128)(2,1)} %weights_ref.1) | copy-start | bytes 393220
  4.3 32.1 %copy-start.1 = (f32[8,128]{1,0:T(8,128)S(1)}, f32[8,128]{1,0:T(8,128)}, u32[]{:S(2)}) copy-start(f32[8,128]{1,0:T(8,128)} %vup_ref.1) | copy-start | bytes 12292
  4.4 32.1 %copy-start.2 = (bf16[8,128]{1,0:T(8,128)(2,1)S(1)}, bf16[8,128]{1,0:T(8,128)(2,1)}, u32[]{:S(2)}) copy-start(bf16[8,128]{1,0:T(8,128)(2,1)} %vectors_ref.1) | copy-start | bytes 6148
  75.4 15.1 %all-to-all-start.2 = ((bf16[128,2,4,128]{3,2,1,0:T(4,128)(2,1)}), bf16[128,2,4,128]{3,2,1,0:T(4,128)(2,1)S(1)}, u32[]{:S(2)}, u32[]{:S(2)}) async-start(bf16[128,2,4,128]{3,2,1,0:T(4,128)(2,1)} %sum_pieces.1), calls=%async_computation.2 | async-start | bytes 524288 | tf_op jit(solution)/shard_map/all_to_all | solution.py:495

commit v3 on v2

--- a/solution.py
+++ b/solution.py
@@ -438,7 +438,7 @@
     msg_ref[:, CUBOIDS + 1] = low_rows.reshape(PEERS, SPAN, CH)
 
 
-def sum_kernel(recv_ref, piece_ref):
+def sum_kernel(recv_ref, piece_hbm, piece_ref, sems):
     summed = jnp.sum(recv_ref[:, CUBOIDS:].astype(F32), axis=0)
     summed = jnp.concatenate([summed[0], summed[1]], axis=0)
     row, slots = vec_slots(PIECE_ROWS)
@@ -453,7 +453,17 @@
     piece = jnp.where(slots, vec, jnp.concatenate([high, weight - high], axis=0))
     for i in range(2):
         rows = piece[i * SPAN : (i + 1) * SPAN].astype(BF)
-        piece_ref[:, i] = jnp.broadcast_to(rows[None], (PEERS, SPAN, CH))
+        piece_ref[:, i] = jnp.broadcast_to(rows[None], (PIECE_GROUP, SPAN, CH))
+    copies = [
+        pltpu.make_async_copy(
+            piece_ref, piece_hbm.at[pl.ds(i * PIECE_GROUP, PIECE_GROUP)], sems.at[i]
+        )
+        for i in range(PEERS // PIECE_GROUP)
+    ]
+    for copy in copies:
+        copy.start()
+    for copy in copies:
+        copy.wait()
 
 
 def spread_kernel(recv_ref, weight_ref, vec_ref):
@@ -534,9 +544,13 @@
     received = exchange(message)
     pieces = pl.pallas_call(
         sum_kernel,
-        out_shape=pltpu.VMEM((PEERS, 2, SPAN, CH), BF),
+        out_shape=jax.ShapeDtypeStruct((PEERS, 2, SPAN, CH), BF),
         in_specs=[VMEM],
-        out_specs=VMEM,
+        out_specs=HBM,
+        scratch_shapes=[
+            pltpu.VMEM((PIECE_GROUP, 2, SPAN, CH), BF),
+            pltpu.SemaphoreType.DMA((PEERS // PIECE_GROUP,)),
+        ],
         compiler_params=PARAMS,
         name="sum_pieces",
     )(received)

time: 91.6 us -> 91.6 us (level)
  no operation moved by 1% of the time
where the time goes in v3:
time: 91.6 us; the launch traced here: 91.4 us
  blocking collectives  52.4 us (57%)
  Pallas kernels  24.4 us (27%)
  waiting for transfers between devices  9.33 us (10%)
  starting transfers between devices  3.83 us (4%)
  between operations  1.35 us (1%)
    all_to_all x2, blocking collectives, exchange(): lax.all_to_all(rows, ('tile', 'frame'), split_axis=0, concat_axis=0, tile...  52.4 us
    pallas_call x1, Pallas kernels, body(): pl.pallas_call(owner_kernel, out_shape=pltpu.VMEM((PEERS, CUBOIDS + 2, SP...  17.5 us
    all_to_all x1, waiting for transfers between devices, exchange(): lax.all_to_all(rows, ('tile', 'frame'), split_axis=0, concat_axis=0, tile...  9.33 us
    all_to_all x1, starting transfers between devices, exchange(): lax.all_to_all(rows, ('tile', 'frame'), split_axis=0, concat_axis=0, tile...  3.83 us
    pallas_call x1, Pallas kernels, body(): pl.pallas_call(pack_kernel, out_shape=pltpu.VMEM((PEERS, MSG_SPANS, SPAN,...  3.05 us
    pallas_call x1, Pallas kernels, body(): pl.pallas_call(place_kernel, out_shape=jax.ShapeDtypeStruct((CELLS_DEV, C...  1.93 us
  transfers between devices with their start and end apart: 1, of which 1 were waited for; matrix products, arithmetic and copies ran while one was open for 0% of the time, Pallas kernels for 2%

profile of v3, /device:TPU:1, one launch (start us, length us, event | category | flops | bytes accessed | tf_op | source)
XLA Modules:
  0.0 91.4 jit_solution(14062404050427311842)
XLA Ops:
  1.3 3.1 %pack.1 = bf16[128,9,4,128]{3,2,1,0:T(4,128)(2,1)S(1)} custom-call(s32[1]{0:T(128)S(6)} %copy.9.shift_hbm, bf16[2048,128]{1,0:T(8,128)(2,1)} %bitcast.4, bf16[2048,128]{1,0:T(8,128)(2,1)} %bitcast.5, bf16[8,128]{1,0:T(8,128)(2,1)} %vectors_ref.1, bf16[4,128,128]{2,1,0:T(8,128)(2,1)} %weights_ref.1, f32[8,128]{1,0:T(8,128)} %vup_ref.1), custom_call_target="tpu_custom_call" | custom-call | tf_op jit(solution)/shard_map/pack/pallas_call | solution.py:509
  4.3 0.0 copy-start
  4.3 0.0 copy-start.1
  4.4 0.0 copy-start.2
  4.4 32.1 %all_to_all.15.recv_ref = bf16[128,9,4,128]{3,2,1,0:T(4,128)(2,1)S(1)} all-to-all(bf16[128,9,4,128]{3,2,1,0:T(4,128)(2,1)S(1)} %pack.1), channel_id=1, replica_groups=mesh['tile'=32,'frame'=4] {'tile','frame'}, dimensions={0} | all-to-all | bytes 2359296 | tf_op jit(solution)/shard_map/all_to_all | solution.py:505
  36.5 0.0 copy-done
  36.5 0.0 copy-done.1
  36.5 0.0 copy-done.2
  36.5 17.5 %owner.1 = bf16[128,6,4,128]{3,2,1,0:T(4,128)(2,1)S(1)} custom-call(bf16[128,9,4,128]{3,2,1,0:T(4,128)(2,1)S(1)} %all_to_all.15.recv_ref, bf16[8,128]{1,0:T(8,128)(2,1)S(1)} %copy-done.2, bf16[4,128,128]{2,1,0:T(8,128)(2,1)S(1)} %copy-done, f32[8,128]{1,0:T(8,128)S(1)} %copy-done.1), custom_call_target="tpu_custom_call" | custom-call | tf_op jit(solution)/shard_map/owner/pallas_call | solution.py:526
  54.0 20.3 %all_to_all.16.recv_ref = bf16[128,6,4,128]{3,2,1,0:T(4,128)(2,1)S(1)} all-to-all(bf16[128,6,4,128]{3,2,1,0:T(4,128)(2,1)S(1)} %owner.1), channel_id=1, replica_groups=mesh['tile'=32,'frame'=4] {'tile','frame'}, dimensions={0} | all-to-all | bytes 1572864 | tf_op jit(solution)/shard_map/all_to_all | solution.py:505
  74.3 1.0 %sum_pieces.1 = bf16[128,2,4,128]{3,2,1,0:T(4,128)(2,1)} custom-call(bf16[128,6,4,128]{3,2,1,0:T(4,128)(2,1)S(1)} %all_to_all.16.recv_ref), custom_call_target="tpu_custom_call" | custom-call | tf_op jit(solution)/shard_map/sum_pieces/pallas_call | solution.py:545
  75.3 3.8 %all-to-all-start.2 = ((bf16[128,2,4,128]{3,2,1,0:T(4,128)(2,1)}), bf16[128,2,4,128]{3,2,1,0:T(4,128)(2,1)S(1)}, u32[]{:S(2)}, u32[]{:S(2)}) async-start(bf16[128,2,4,128]{3,2,1,0:T(4,128)(2,1)} %sum_pieces.1), calls=%async_computation.2 | async-start | bytes 524288 | tf_op jit(solution)/shard_map/all_to_all | solution.py:505
  79.2 1.9 %place.1 = bf16[2048,128]{1,0:T(8,128)(2,1)} custom-call(s32[1]{0:T(128)S(6)} %copy.9.shift_hbm, bf16[128,6,4,128]{3,2,1,0:T(4,128)(2,1)S(1)} %all_to_all.16.recv_ref), custom_call_target="tpu_custom_call" | custom-call | tf_op jit(solution)/shard_map/place/pallas_call | solution.py:558
  81.1 9.3 %all-to-all-done.2.recv_ref = bf16[128,2,4,128]{3,2,1,0:T(4,128)(2,1)S(1)} async-done(((bf16[128,2,4,128]{3,2,1,0:T(4,128)(2,1)}), bf16[128,2,4,128]{3,2,1,0:T(4,128)(2,1)S(1)}, u32[]{:S(2)}, u32[]{:S(2)}) %all-to-all-start.2) | async-done | bytes 262176 | tf_op jit(solution)/shard_map/all_to_all | solution.py:505
  90.4 0.9 %spread.1 = (f32[4,128,128]{2,1,0:T(8,128)}, f32[8,128]{1,0:T(8,128)}) custom-call(bf16[128,2,4,128]{3,2,1,0:T(4,128)(2,1)S(1)} %all-to-all-done.2.recv_ref), custom_call_target="tpu_custom_call" | custom-call | tf_op jit(solution)/shard_map/spread/pallas_call | solution.py:571
Async XLA Ops:
  4.3 32.1 %copy-start = (bf16[4,128,128]{2,1,0:T(8,128)(2,1)S(1)}, bf16[4,128,128]{2,1,0:T(8,128)(2,1)}, u32[]{:S(2)}) copy-start(bf16[4,128,128]{2,1,0:T(8,128)(2,1)} %weights_ref.1) | copy-start | bytes 393220
  4.3 32.1 %copy-start.1 = (f32[8,128]{1,0:T(8,128)S(1)}, f32[8,128]{1,0:T(8,128)}, u32[]{:S(2)}) copy-start(f32[8,128]{1,0:T(8,128)} %vup_ref.1) | copy-start | bytes 12292
  4.4 32.1 %copy-start.2 = (bf16[8,128]{1,0:T(8,128)(2,1)S(1)}, bf16[8,128]{1,0:T(8,128)(2,1)}, u32[]{:S(2)}) copy-start(bf16[8,128]{1,0:T(8,128)(2,1)} %vectors_ref.1) | copy-start | bytes 6148
  75.3 15.1 %all-to-all-start.2 = ((bf16[128,2,4,128]{3,2,1,0:T(4,128)(2,1)}), bf16[128,2,4,128]{3,2,1,0:T(4,128)(2,1)S(1)}, u32[]{:S(2)}, u32[]{:S(2)}) async-start(bf16[128,2,4,128]{3,2,1,0:T(4,128)(2,1)} %sum_pieces.1), calls=%async_computation.2 | async-start | bytes 524288 | tf_op jit(solution)/shard_map/all_to_all | solution.py:505
